TPU v7x, 32 devices: a whole 2x2x4 slice. The times are simulated.
32 devices in a mesh: dp: 4 (over y, x), seq: 8 (over z, core).
Axes of the slice: x: 2, y: 2, z: 4, core: 2. Of those that a mesh axis runs over, the one named last changes fastest.
Arguments:
- queries: bfloat16 [4096, 32, 128], P(('dp', 'seq')), parts along dimension 0, may hold values from -6 to 6
- keys: bfloat16 [4096, 4, 128], P(('dp', 'seq')), parts along dimension 0, may hold values from -6 to 6
- values: bfloat16 [4096, 4, 128], P(('dp', 'seq')), parts along dimension 0, may hold values from -6 to 6
- attn_out: bfloat16 [4096, 32, 128], P(('dp', 'seq')), parts along dimension 0, may hold values from -6 to 6
- out_grad: bfloat16 [4096, 32, 128], P(('dp', 'seq')), parts along dimension 0, may hold values from -1.5 to 1.5
- log_sums: float32 [32, 4096], P(None, ('dp', 'seq')), parts along dimension 1, may hold values from 2 to 4
- doc_ids: int32 [4096], P('dp'), parts along dimension 0, may hold values from 0 to 3, never falling along the last dimension, each value on 1 to 512 neighbouring positions
Outputs:
- query_grad: bfloat16 [4096, 32, 128], P(('dp', 'seq')), parts along dimension 0
- key_grad: bfloat16 [4096, 4, 128], P(('dp', 'seq')), parts along dimension 0
- value_grad: bfloat16 [4096, 4, 128], P(('dp', 'seq')), parts along dimension 0
There are 4 independent parts, one for each index of `dp`. A program takes and returns all parts, laid end to end along the dimension named above; each array names one. Nothing has to cross between parts.
Inputs may be any that keep to these rules, and one draw needn't show every extreme that they name: `doc_ids`: document numbers never fall along the sequence; each document holds 1 to 512 positions, and one holds exactly 512.
All inputs are finite; a program needn't handle non-finite values.
Results may differ from a plain program's by a relative error of at most 0.009.
Values may be sent and summed in bfloat16 or wider, within the bound.
No kernel may reach another device: no remote copies, remote signals or barrier semaphores. Data moves between devices by JAX's collectives and lax.ppermute only.
A program may use at most 64 MiB of HBM per device.

v0:
```python
import functools

import jax
import jax.numpy as jnp
from jax import lax
from jax.experimental import pallas as pl
from jax.experimental.pallas import tpu as pltpu
from jax.sharding import PartitionSpec as P

COSTS = {
    "pack": 10,
    "prep_early": 10,
    "prep_late": 10,
    "near_early": 10,
    "mid_even": 10,
    "mid_odd": 10,
    "far": 10,
    "near": 10,
    "query_own": 10,
    "sums": 10,
}
EARLY_HEADS = 4
LOG2E = 1.4426950408889634
HBM = pl.BlockSpec(memory_space=pltpu.HBM)
VMEM = pl.BlockSpec(memory_space=pltpu.VMEM)
NT = (((1,), (1,)), ((), ()))
TN = (((0,), (0,)), ((), ()))
BF = jnp.bfloat16
F32 = jnp.float32


def call(kernel, name, shapes, operands, specs=None, scratch=(), after=(), mib=8, aliases=None):
    count = len(operands)

    def run(*refs):
        kernel(*refs[:count], *refs[count + len(after) :])

    return pl.pallas_call(
        run,
        in_specs=(specs or [VMEM] * count) + [VMEM] * len(after),
        out_specs=[VMEM] * len(shapes),
        out_shape=[jax.ShapeDtypeStruct(*one) for one in shapes],
        scratch_shapes=scratch,
        compiler_params=pltpu.CompilerParams(vmem_limit_bytes=mib * 1024 * 1024),
        cost_estimate=pl.CostEstimate(flops=int(COSTS[name] * 1e9), bytes_accessed=10**7, transcendentals=0),
        input_output_aliases=aliases or {},
        name=name,
    )(*operands, *after)


def split3(value):
    high = value.astype(BF).astype(F32)
    rest = value - high
    middle = rest.astype(BF).astype(F32)
    return high, middle, rest - middle


def start_copies(pairs, sems):
    copies = []
    for i, (source, target) in enumerate(pairs):
        copies.append(pltpu.make_async_copy(source, target, sems.at[i]))
        copies[-1].start()
    return copies


def pack_kernel(k_hbm, v_hbm, all_ref, k_ref, v_ref, sems):
    copies = start_copies(((k_hbm, k_ref), (v_hbm, v_ref)), sems)
    kv_count = k_ref.shape[1]
    for i, ref in enumerate((k_ref, v_ref)):
        copies[i].wait()
        for kv in range(kv_count):
            all_ref[i * kv_count + kv] = ref[:, kv, :]


def prep_kernel(q_hbm, g_hbm, o_hbm, log_hbm, q1_ref, g1_ref, o1_ref, log1_ref, *refs):
    rows_ref, sub_ref, q_ref, g_ref, o_ref, log_ref, log_sem, sems = refs
    rows, heads, size = q_ref.shape
    kv_count = rows_ref.shape[2]
    group = heads // kv_count
    step = 32
    log_copy = start_copies(((log_hbm, log_ref),), log_sem)[0]
    copies = []
    for i, at in enumerate(range(0, rows, step)):
        part = pl.ds(at, step)
        pairs = [(one.at[part], two.at[part]) for one, two in ((g_hbm, g_ref), (o_hbm, o_ref), (q_hbm, q_ref))]
        copies.append(start_copies(pairs, sems.at[i]))
    lane_row = lax.broadcasted_iota(jnp.int32, (rows, 128), 1)
    lane = lax.broadcasted_iota(jnp.int32, (1, heads, 128), 2)
    head = lax.broadcasted_iota(jnp.int32, (1, heads, 128), 1)
    own = (lane == head) | (lane == head + heads) | (lane == head + 2 * heads)
    ones = jnp.where(lax.broadcasted_iota(jnp.int32, (128, 128), 0) < 3 * heads, 1.0, 0.0).astype(BF)
    for side, (q_one, g_one, o_one, log_one) in (
        (1, (q1_ref, g1_ref, o1_ref, log1_ref)),
        (0, (q_ref, g_ref, o_ref, log_ref)),
    ):
        if side == 0:
            log_copy.wait()
        logs = jnp.concatenate([log_one[...] * LOG2E] * (128 // heads), axis=0).T
        l_high, l_mid, l_low = split3(logs)
        logs = jnp.where(lane_row < heads, l_high, jnp.where(lane_row < 2 * heads, l_mid, l_low))
        for i, at in enumerate(range(0, rows, step)):
            part = slice(at, at + step)
            if side == 0:
                for one in copies[i]:
                    one.wait()
            grad, query = g_one[part], q_one[part]
            delta = jnp.sum(grad.astype(F32) * o_one[part].astype(F32), axis=-1, keepdims=True)
            delta = jnp.broadcast_to(delta, (step, heads, 128))
            aux = jnp.where(own, logs[part, None, :], 0.0).astype(BF)
            spot = slice(at * group, (at + step) * group)
            for kv in range(kv_count):
                span = slice(kv * group, (kv + 1) * group)
                rows_ref[side, 0, kv, spot] = query[:, span, :].reshape(step * group, size)
                rows_ref[side, 1, kv, spot] = grad[:, span, :].reshape(step * group, size)
                sub_ref[side, 0, kv, spot] = jnp.dot(
                    aux[:, span, :].reshape(step * group, 128), ones, preferred_element_type=F32
                )
                sub_ref[side, 1, kv, spot] = delta[:, span, :].reshape(step * group, 128)


def sends_far():
    return lax.axis_index("seq") + 4 < lax.axis_size("seq")


def prep_early_kernel(*refs):
    @pl.when(sends_far())
    def _():
        prep_kernel(*refs)


def prep_late_kernel(doc_ref, *refs):
    ends_ref = refs[12]
    for step in range(3):
        for side in range(2):
            at = 2 * step + side
            ends_ref[at : at + 1, :] = ends_of(doc_ref, 2 * step, side)

    @pl.when(jnp.logical_not(sends_far()))
    def _():
        prep_kernel(*refs[:8], *refs[10:12], *refs[13:])


def mid_kernel(parity, *refs):
    @pl.when((lax.axis_index("seq") // 2) % 2 == parity)
    def _():
        chunk_kernel(2, *refs[:4], *refs[-3:])


def ends_of(doc_ref, distance, side):
    rows = doc_ref.shape[1]
    shard = lax.axis_index("seq")
    key_shard, query_shard = shard - distance, shard ^ side
    key_doc = doc_ref[pl.ds(jnp.maximum(key_shard, 0), 1), :]
    query_rows = jnp.broadcast_to(doc_ref[pl.ds(query_shard, 1), :], (rows, rows)).T
    ends = jnp.sum((query_rows <= key_doc).astype(jnp.int32), axis=0, keepdims=True)
    return jnp.where((key_shard >= 0) & (key_shard <= query_shard), ends, 0)


def chunk_kernel(distance, ends_ref, rows_ref, sub_ref, kv_ref, ds_ref, out_ref, acc, early=None):
    count, size = rows_ref.shape[3:]
    each, width = kv_ref.shape[0] // 2, kv_ref.shape[1]
    rows = width
    scale = size ** (-0.5)
    shard = lax.axis_index("seq")
    key_shard = shard - distance
    if early is None:
        acc[...] = jnp.zeros_like(acc)
    for side in range(2):
        query_shard = shard ^ side
        if early == "only":
            ends = ends_of(ends_ref, distance, side)
        else:
            ends = ends_ref[distance + side : distance + side + 1, :]
        live = jnp.max(ends) > 0

        def heads(these):
            pos = lax.broadcasted_iota(jnp.int32, (rows, count // rows, width), 0).reshape(count, width)
            low = (key_shard - query_shard) * width + lax.broadcasted_iota(jnp.int32, (1, width), 1)
            mask = (pos >= low) & (pos < ends)
            for j in these:
                query, grad = rows_ref[side, 0, j], rows_ref[side, 1, j]
                logits = lax.dot_general(query, kv_ref[j], NT, preferred_element_type=F32)
                logits = logits * (scale * LOG2E) - sub_ref[side, 0, j]
                probs = jnp.where(mask, jnp.exp2(logits), 0.0)
                diff = lax.dot_general(grad, kv_ref[each + j], NT, preferred_element_type=F32)
                ds = (probs * (diff - sub_ref[side, 1, j])).astype(BF)
                ds_ref[side, j] = ds
                sums = lax.dot_general(
                    jnp.concatenate([ds, probs.astype(BF)], axis=1),
                    jnp.concatenate([query, grad], axis=1),
                    TN,
                    preferred_element_type=F32,
                )
                acc[j] += sums[:width, :size] * scale
                acc[each + j] += sums[width:, size:]

        if early == "only":
            if side == 0:
                heads(range(EARLY_HEADS))
            continue
        if early == "rest" and side == 0:
            pl.when(jnp.logical_not(sends_far()))(functools.partial(heads, range(EARLY_HEADS)))
            heads(range(EARLY_HEADS, each))
            continue
        pl.when(live)(functools.partial(heads, range(each)))

        @pl.when(jnp.logical_not(live))
        def _():
            ds_ref[side] = jnp.zeros(ds_ref.shape[1:], BF)

    out_ref[...] = acc[...].astype(out_ref.dtype)


def query_kernel(side, ds0_ref, ds1_ref, ds2_ref, kv0_ref, kv1_ref, kv2_ref, out_ref):
    rows, heads, size = out_ref.shape
    kv_count = kv0_ref.shape[0] // 2
    group = heads // kv_count
    for kv in range(kv_count):
        ds = jnp.concatenate([one[side, kv] for one in (ds0_ref, ds1_ref, ds2_ref)], axis=1)
        key = jnp.concatenate([one[kv] for one in (kv0_ref, kv1_ref, kv2_ref)], axis=0)
        got = jnp.dot(ds, key, preferred_element_type=F32) * size ** (-0.5)
        out_ref[:, kv * group : (kv + 1) * group, :] = got.reshape(rows, group, size).astype(out_ref.dtype)


def near_early_kernel(doc_ref, rows_ref, sub_ref, kv_ref, copy_ref, ds_ref, acc):
    copy_ref[...] = kv_ref[...]

    @pl.when(sends_far())
    def _():
        acc[...] = jnp.zeros_like(acc)
        chunk_kernel(0, doc_ref, rows_ref, sub_ref, kv_ref, ds_ref, acc, acc, "only")


def near_kernel(
    doc_ref, rows_ref, sub_ref, kv_ref, _, sums_in, ds1_ref, ds2_ref, kv1_ref, kv2_ref, ds_ref, out_ref, query_ref, acc
):
    acc[...] = jnp.zeros_like(acc)

    @pl.when(sends_far())
    def _():
        acc[...] = sums_in[...]

    chunk_kernel(0, doc_ref, rows_ref, sub_ref, kv_ref, ds_ref, out_ref, acc, "rest")
    query_kernel(1, ds_ref, ds1_ref, ds2_ref, kv_ref, kv1_ref, kv2_ref, query_ref)


def sum_kernel(one_ref, two_ref, sums_ref, query_ref, key_ref, val_ref):
    query_ref[...] = (one_ref[...] + two_ref[...].astype(F32)).astype(BF)
    kv_count = key_ref.shape[1]
    for i, ref in enumerate((key_ref, val_ref)):
        heads = [sums_ref[i * kv_count + kv] for kv in range(kv_count)]
        ref[...] = jnp.stack(heads, axis=1).astype(BF)


def on_device(queries, keys, values, attn_out, out_grad, log_sums, doc_ids):
    width, heads, size = queries.shape
    kv_count = keys.shape[1]
    count = lax.axis_size("seq")
    docs = doc_ids.reshape(-1, width)
    rows = width * heads // kv_count
    full = (2 * kv_count, width, size)

    def flip(value):
        return lax.ppermute(value, "seq", [(i, i ^ 1) for i in range(count)])

    def move(value, steps, parity=None):
        pairs = [(i, i + steps) for i in range(count) if 0 <= i + steps < count]
        return lax.ppermute(value, "seq", [one for one in pairs if parity in (None, one[0] // 2 % 2)])

    hbm = functools.partial(pltpu.with_memory_space_constraint, memory_space=pltpu.HBM)
    (near,) = call(
        pack_kernel,
        "pack",
        [(full, BF)],
        (hbm(keys), hbm(values)),
        specs=[HBM] * 2,
        scratch=[pltpu.VMEM(keys.shape, BF)] * 2 + [pltpu.SemaphoreType.DMA((2,))],
    )
    mid = move(near, 2)
    own = (queries, out_grad, attn_out, log_sums)
    own = tuple(hbm(one) for one in own) + tuple(flip(one) for one in own)
    laid = [((2, 2, kv_count, rows, size), BF), ((2, 2, kv_count, rows, 128), F32)]
    prep = dict(
        specs=[HBM] * 4 + [VMEM] * 4,
        scratch=[pltpu.VMEM(queries.shape, BF)] * 3
        + [pltpu.VMEM(log_sums.shape, F32)]
        + [pltpu.SemaphoreType.DMA((1,)), pltpu.SemaphoreType.DMA((width // 32, 3))],
        mib=24,
    )
    lay, sub = call(prep_early_kernel, "prep_early", laid, own, **prep)
    copied, ds_near, near_sums = call(
        near_early_kernel,
        "near_early",
        [(full, BF), ((2, kv_count, rows, width), BF), (full, F32)],
        (docs, lay, sub, near),
    )
    far = move(copied, 4)
    prep["specs"] = [VMEM] + [HBM] * 4 + [VMEM] * 6
    lay, sub, ends = call(
        prep_late_kernel,
        "prep_late",
        [*laid, ((8, width), jnp.int32)],
        (docs, *own, lay, sub),
        aliases={9: 0, 10: 1},
        **prep,
    )

    def chunk(kv, distance, name, after=()):
        return call(
            functools.partial(chunk_kernel, distance),
            name,
            [((2, kv_count, rows, width), BF), (full, BF)],
            (ends, lay, sub, kv),
            scratch=[pltpu.VMEM(full, F32)],
            after=after,
        )

    mid_shapes = [((2, kv_count, rows, width), BF), (full, BF)]
    mid_scratch = [pltpu.VMEM(full, F32)]
    ds_mid, even_sums = call(
        functools.partial(mid_kernel, 0), "mid_even", mid_shapes, (ends, lay, sub, mid), scratch=mid_scratch
    )
    even_back = move(even_sums, -2, 0)
    ds_mid, odd_sums = call(
        functools.partial(mid_kernel, 1),
        "mid_odd",
        mid_shapes,
        (ends, lay, sub, mid, ds_mid),
        scratch=mid_scratch,
        aliases={4: 0},
    )
    odd_back = move(odd_sums, -2, 1)
    ds_far, far_sums = chunk(far, 4, "far", (ds_mid,))
    far_back = move(far_sums, -4)
    ds_near, near_sums, part = call(
        near_kernel,
        "near",
        [((2, kv_count, rows, width), BF), (full, F32), (queries.shape, BF)],
        (ends, lay, sub, near, ds_near, near_sums, ds_mid, ds_far, mid, far),
        scratch=[pltpu.VMEM(full, F32)],
        aliases={4: 0},
        after=(even_back,),
    )
    (mine,) = call(
        functools.partial(query_kernel, 0),
        "query_own",
        [(queries.shape, F32)],
        (ds_near, ds_mid, ds_far, near, mid, far),
    )
    sums = near_sums + even_back.astype(F32) + odd_back.astype(F32) + far_back.astype(F32)
    query_grad, key_grad, val_grad = call(
        sum_kernel,
        "sums",
        [(queries.shape, BF)] + [(keys.shape, BF)] * 2,
        (mine, flip(part), sums),
    )
    return query_grad, key_grad, val_grad


def solution(mesh):
    rows = P(("dp", "seq"), None, None)
    return jax.shard_map(
        on_device,
        mesh=mesh,
        in_specs=(rows,) * 5 + (P(None, ("dp", "seq")), P("dp")),
        out_specs=(rows,) * 3,
        check_vma=False,
    )
```

profile of v0, /device:TPU:10, one launch (start us, length us, event | category | flops | bytes accessed | tf_op | source)
XLA Modules:
  0.0 37.6 jit_solution(6620894573005225763)
XLA Ops:
  0.6 0.1 collective-permute-start
  0.7 0.5 %collective-permute-start.1 = (bf16[128,32,128]{2,1,0:T(8,128)(2,1)}, bf16[128,32,128]{2,1,0:T(8,128)(2,1)S(1)}, u32[]{:S(2)}, u32[]{:S(2)}) collective-permute-start(bf16[128,32,128]{2,1,0:T(8,128)(2,1)} %refs_2_.3), channel_id=1, source_target_pairs={{0,1},{1,0},{2,3},{3,2},{4,5},{5,4},{6,7},{7,6},{8,9},{9,8},{10,11... | collective-permute-start | bytes 3145736 | tf_op jit(solution)/shard_map/ppermute | solution.py:264
  1.2 0.1 collective-permute-start.2
  1.3 0.4 %collective-permute-start.3 = (f32[32,128]{1,0:T(8,128)}, f32[32,128]{1,0:T(8,128)S(1)}, u32[]{:S(2)}, u32[]{:S(2)}) collective-permute-start(f32[32,128]{1,0:T(8,128)} %refs_4_.1), channel_id=1, source_target_pairs={{0,1},{1,0},{2,3},{3,2},{4,5},{5,4},{6,7},{7,6},{8,9},{9,8},{10,11... | collective-permute-start | bytes 49160 | tf_op jit(solution)/shard_map/ppermute | solution.py:264
  1.7 1.5 %pack.1.refs_3_ = bf16[8,128,128]{2,1,0:T(8,128)(2,1)S(1)} custom-call(bf16[128,4,128]{2,1,0:T(4,128)(2,1)} %refs_0_.3, bf16[128,4,128]{2,1,0:T(4,128)(2,1)} %refs_1_.5), custom_call_target="tpu_custom_call" | custom-call | flops 10000000000 | bytes 10000000 | tf_op jit(solution)/shard_map/pack/pallas_call | solution.py:38
  3.3 0.0 copy-start
  3.3 3.5 %collective-permute-start.4 = (bf16[8,128,128]{2,1,0:T(8,128)(2,1)S(1)}, bf16[8,128,128]{2,1,0:T(8,128)(2,1)S(1)}, u32[]{:S(2)}, u32[]{:S(2)}) collective-permute-start(bf16[8,128,128]{2,1,0:T(8,128)(2,1)S(1)} %pack.1.refs_3_), channel_id=1, source_target_pairs={{0,2},{1,3},{2,4},{3,5},{4,6},{5,7},{8,10},{9,11},{10,12},{11,13},... | collective-permute-start | bytes 786440 | tf_op jit(solution)/shard_map/ppermute | solution.py:268
  6.8 0.0 collective-permute-done.3.refs_7_.refs_8_
  6.8 0.0 collective-permute-done.refs_4_.refs_5_
  6.8 0.0 collective-permute-done.1.refs_5_.refs_6_
  6.8 0.0 collective-permute-done.2.refs_6_.refs_7_
  6.8 2.9 %prep_early.1 = (bf16[2,2,4,1024,128]{4,3,2,1,0:T(8,128)(2,1)S(1)}, f32[2,2,4,1024,128]{4,3,2,1,0:T(8,128)S(1)}) custom-call(bf16[128,32,128]{2,1,0:T(8,128)(2,1)} %refs_1_.4, bf16[128,32,128]{2,1,0:T(8,128)(2,1)} %refs_2_.3, bf16[128,32,128]{2,1,0:T(8,128)(2,1)} %refs_3_.3, f32[32,128]{1,0:T(8,128)} %refs_4_.1, ...), custom_call_target="tpu_custom_call" | custom-call | flops 10000000000 | bytes 10000000 | tf_op jit(solution)/shard_map/prep_early/pallas_call | solution.py:38
  9.7 0.0 copy-done
  9.7 1.7 %near_early.1 = (bf16[8,128,128]{2,1,0:T(8,128)(2,1)S(1)}, bf16[2,4,1024,128]{3,2,1,0:T(8,128)(2,1)S(1)}, f32[8,128,128]{2,1,0:T(8,128)S(1)}) custom-call(s32[8,128]{1,0:T(8,128)S(1)} %bitcast.1, bf16[2,2,4,1024,128]{4,3,2,1,0:T(8,128)(2,1)S(1)} %get-tuple-element.20.refs_9_.refs_1_, f32[2,2,4,1024,128]{4,3,2,1,0:T(8,128)S(1)} %get-tuple-element.21.refs_10_.refs_2_, ...), custom_call_target="tpu_custom_call" | custom-call | flops 10000000000 | bytes 10000000 | tf_op jit(solution)/shard_map/near_early/pallas_call | solution.py:38
  11.4 1.3 %collective-permute-start.5 = (bf16[8,128,128]{2,1,0:T(8,128)(2,1)S(1)}, bf16[8,128,128]{2,1,0:T(8,128)(2,1)S(1)}, u32[]{:S(2)}, u32[]{:S(2)}) collective-permute-start(bf16[8,128,128]{2,1,0:T(8,128)(2,1)S(1)} %get-tuple-element.29), channel_id=1, source_target_pairs={{0,4},{1,5},{2,6},{3,7},{8,12},{9,13},{10,14},{11,15},{16,20},{17,... | collective-permute-start | bytes 786440 | tf_op jit(solution)/shard_map/ppermute | solution.py:268
  12.7 0.3 prep_late.1
  13.0 0.5 %collective-permute-done.4.refs_3_.refs_8_.refs_4_ = bf16[8,128,128]{2,1,0:T(8,128)(2,1)S(1)} collective-permute-done((bf16[8,128,128]{2,1,0:T(8,128)(2,1)S(1)}, bf16[8,128,128]{2,1,0:T(8,128)(2,1)S(1)}, u32[]{:S(2)}, u32[]{:S(2)}) %collective-permute-start.4) | collective-permute-done | bytes 262176 | tf_op jit(solution)/shard_map/ppermute | solution.py:268
  13.5 1.3 %collective-permute-start.6 = (bf16[8,128,128]{2,1,0:T(8,128)(2,1)S(1)}, bf16[8,128,128]{2,1,0:T(8,128)(2,1)S(1)}, u32[]{:S(2)}, u32[]{:S(2)}) collective-permute-start(bf16[8,128,128]{2,1,0:T(8,128)(2,1)S(1)} %get-tuple-element.31), channel_id=1, source_target_pairs={{4,2},{5,3},{12,10},{13,11},{20,18},{21,19},{28,26},{29,27}} | collective-permute-start | bytes 786440 | tf_op jit(solution)/shard_map/ppermute | solution.py:268
  14.8 3.9 %mid_odd.1 = (bf16[2,4,1024,128]{3,2,1,0:T(8,128)(2,1)S(1)}, bf16[8,128,128]{2,1,0:T(8,128)(2,1)S(1)}) custom-call(s32[8,128]{1,0:T(8,128)S(1)} %get-tuple-element.22.refs_0_, bf16[2,2,4,1024,128]{4,3,2,1,0:T(8,128)(2,1)S(1)} %get-tuple-element.23.refs_1_, f32[2,2,4,1024,128]{4,3,2,1,0:T(8,128)S(1)} %get-tuple-element.24.refs_2_, ...), custom_call_target="tpu_custom_call", output_to_operand_aliasing={{0}: (4, {})} | custom-call | flops 10000000000 | bytes 10000000 | tf_op jit(solution)/shard_map/mid_odd/pallas_call | solution.py:38
  18.7 1.3 %collective-permute-start.8 = (bf16[8,128,128]{2,1,0:T(8,128)(2,1)S(1)}, bf16[8,128,128]{2,1,0:T(8,128)(2,1)S(1)}, u32[]{:S(2)}, u32[]{:S(2)}) collective-permute-start(bf16[8,128,128]{2,1,0:T(8,128)(2,1)S(1)} %get-tuple-element.35), channel_id=1, source_target_pairs={{2,0},{3,1},{6,4},{7,5},{10,8},{11,9},{14,12},{15,13},{18,16},{19,... | collective-permute-start | bytes 786440 | tf_op jit(solution)/shard_map/ppermute | solution.py:268
  20.0 4.1 %collective-permute-done.5.refs_3_.refs_9_.refs_5_ = bf16[8,128,128]{2,1,0:T(8,128)(2,1)S(1)} collective-permute-done((bf16[8,128,128]{2,1,0:T(8,128)(2,1)S(1)}, bf16[8,128,128]{2,1,0:T(8,128)(2,1)S(1)}, u32[]{:S(2)}, u32[]{:S(2)}) %collective-permute-start.5) | collective-permute-done | bytes 262176 | tf_op jit(solution)/shard_map/ppermute | solution.py:268
  24.1 0.7 %far.1 = (bf16[2,4,1024,128]{3,2,1,0:T(8,128)(2,1)S(1)}, bf16[8,128,128]{2,1,0:T(8,128)(2,1)S(1)}) custom-call(s32[8,128]{1,0:T(8,128)S(1)} %get-tuple-element.22.refs_0_, bf16[2,2,4,1024,128]{4,3,2,1,0:T(8,128)(2,1)S(1)} %get-tuple-element.23.refs_1_, f32[2,2,4,1024,128]{4,3,2,1,0:T(8,128)S(1)} %get-tuple-element.24.refs_2_, ...), custom_call_target="tpu_custom_call" | custom-call | flops 10000000000 | bytes 10000000 | tf_op jit(solution)/shard_map/far/pallas_call | solution.py:38
  24.8 1.3 %collective-permute-start.9 = (bf16[8,128,128]{2,1,0:T(8,128)(2,1)S(1)}, bf16[8,128,128]{2,1,0:T(8,128)(2,1)S(1)}, u32[]{:S(2)}, u32[]{:S(2)}) collective-permute-start(bf16[8,128,128]{2,1,0:T(8,128)(2,1)S(1)} %get-tuple-element.36), channel_id=1, source_target_pairs={{4,0},{5,1},{6,2},{7,3},{12,8},{13,9},{14,10},{15,11},{20,16},{21,... | collective-permute-start | bytes 786440 | tf_op jit(solution)/shard_map/ppermute | solution.py:268
  26.1 0.0 collective-permute-done.6.refs_10_
  26.1 2.9 %near.1 = (bf16[2,4,1024,128]{3,2,1,0:T(8,128)(2,1)S(1)}, f32[8,128,128]{2,1,0:T(8,128)S(1)}, bf16[128,32,128]{2,1,0:T(8,128)(2,1)S(1)}) custom-call(s32[8,128]{1,0:T(8,128)S(1)} %get-tuple-element.22.refs_0_, bf16[2,2,4,1024,128]{4,3,2,1,0:T(8,128)(2,1)S(1)} %get-tuple-element.23.refs_1_, ...), custom_call_target="tpu_custom_call", output_to_operand_aliasing={{0}: (4, {})} | custom-call | flops 10000000000 | bytes 10000000 | tf_op jit(solution)/shard_map/near/pallas_call | solution.py:38
  29.1 0.1 collective-permute-start.7
  29.1 1.0 %query_own.1.refs_0_ = f32[128,32,128]{2,1,0:T(8,128)S(1)} custom-call(bf16[2,4,1024,128]{3,2,1,0:T(8,128)(2,1)S(1)} %get-tuple-element.32.refs_0_, bf16[2,4,1024,128]{3,2,1,0:T(8,128)(2,1)S(1)} %get-tuple-element.28.refs_4_.refs_6_.refs_1_, bf16[2,4,1024,128]{3,2,1,0:T(8,128)(2,1)S(1)} %get-tuple-element.30.refs_7_.refs_2_, ...), custom_call_target="tpu_custom_call" | custom-call | flops 10000000000 | bytes 10000000 | tf_op jit(solution)/shard_map/query_own/pallas_call | solution.py:38
  30.1 1.0 %collective-permute-done.8 = bf16[8,128,128]{2,1,0:T(8,128)(2,1)S(1)} collective-permute-done((bf16[8,128,128]{2,1,0:T(8,128)(2,1)S(1)}, bf16[8,128,128]{2,1,0:T(8,128)(2,1)S(1)}, u32[]{:S(2)}, u32[]{:S(2)}) %collective-permute-start.8) | collective-permute-done | bytes 262176 | tf_op jit(solution)/shard_map/ppermute | solution.py:268
  31.1 4.9 %collective-permute-done.9 = bf16[8,128,128]{2,1,0:T(8,128)(2,1)S(1)} collective-permute-done((bf16[8,128,128]{2,1,0:T(8,128)(2,1)S(1)}, bf16[8,128,128]{2,1,0:T(8,128)(2,1)S(1)}, u32[]{:S(2)}, u32[]{:S(2)}) %collective-permute-start.9) | collective-permute-done | bytes 262176 | tf_op jit(solution)/shard_map/ppermute | solution.py:268
  36.0 0.1 convert_add_fusion.refs_2_
  36.1 0.0 collective-permute-done.7.refs_1_
  36.1 1.5 %sums.1 = (bf16[128,32,128]{2,1,0:T(8,128)(2,1)}, bf16[128,4,128]{2,1,0:T(4,128)(2,1)}, bf16[128,4,128]{2,1,0:T(4,128)(2,1)}) custom-call(f32[128,32,128]{2,1,0:T(8,128)S(1)} %query_own.1.refs_0_, bf16[128,32,128]{2,1,0:T(8,128)(2,1)S(1)} %collective-permute-done.7.refs_1_, f32[8,128,128]{2,1,0:T(8,128)S(1)} %convert_add_fusion.refs_2_), custom_call_target="tpu_custom_call" | custom-call | flops 10000000000 | bytes 10000000 | tf_op jit(solution)/shard_map/sums/pallas_call | solution.py:38
  (1 shorter events, 0.0 us)
Async XLA Ops:
  0.6 6.2 %collective-permute-start = (bf16[128,32,128]{2,1,0:T(8,128)(2,1)}, bf16[128,32,128]{2,1,0:T(8,128)(2,1)S(1)}, u32[]{:S(2)}, u32[]{:S(2)}) collective-permute-start(bf16[128,32,128]{2,1,0:T(8,128)(2,1)} %refs_1_.4), channel_id=1, source_target_pairs={{0,1},{1,0},{2,3},{3,2},{4,5},{5,4},{6,7},{7,6},{8,9},{9,8},{10,11... | collective-permute-start | bytes 3145736 | tf_op jit(solution)/shard_map/ppermute | solution.py:264
  0.7 6.1 %collective-permute-start.1 = (bf16[128,32,128]{2,1,0:T(8,128)(2,1)}, bf16[128,32,128]{2,1,0:T(8,128)(2,1)S(1)}, u32[]{:S(2)}, u32[]{:S(2)}) collective-permute-start(bf16[128,32,128]{2,1,0:T(8,128)(2,1)} %refs_2_.3), channel_id=1, source_target_pairs={{0,1},{1,0},{2,3},{3,2},{4,5},{5,4},{6,7},{7,6},{8,9},{9,8},{10,11... | collective-permute-start | bytes 3145736 | tf_op jit(solution)/shard_map/ppermute | solution.py:264
  1.2 5.6 %collective-permute-start.2 = (bf16[128,32,128]{2,1,0:T(8,128)(2,1)}, bf16[128,32,128]{2,1,0:T(8,128)(2,1)S(1)}, u32[]{:S(2)}, u32[]{:S(2)}) collective-permute-start(bf16[128,32,128]{2,1,0:T(8,128)(2,1)} %refs_3_.3), channel_id=1, source_target_pairs={{0,1},{1,0},{2,3},{3,2},{4,5},{5,4},{6,7},{7,6},{8,9},{9,8},{10,11... | collective-permute-start | bytes 3145736 | tf_op jit(solution)/shard_map/ppermute | solution.py:264
  1.3 5.5 %collective-permute-start.3 = (f32[32,128]{1,0:T(8,128)}, f32[32,128]{1,0:T(8,128)S(1)}, u32[]{:S(2)}, u32[]{:S(2)}) collective-permute-start(f32[32,128]{1,0:T(8,128)} %refs_4_.1), channel_id=1, source_target_pairs={{0,1},{1,0},{2,3},{3,2},{4,5},{5,4},{6,7},{7,6},{8,9},{9,8},{10,11... | collective-permute-start | bytes 49160 | tf_op jit(solution)/shard_map/ppermute | solution.py:264
  3.3 6.4 %copy-start = (s32[1024]{0:T(1024)S(1)}, s32[1024]{0:T(1024)}, u32[]{:S(2)}) copy-start(s32[1024]{0:T(1024)} %param.13) | copy-start | bytes 12292
  3.3 10.2 %collective-permute-start.4 = (bf16[8,128,128]{2,1,0:T(8,128)(2,1)S(1)}, bf16[8,128,128]{2,1,0:T(8,128)(2,1)S(1)}, u32[]{:S(2)}, u32[]{:S(2)}) collective-permute-start(bf16[8,128,128]{2,1,0:T(8,128)(2,1)S(1)} %pack.1.refs_3_), channel_id=1, source_target_pairs={{0,2},{1,3},{2,4},{3,5},{4,6},{5,7},{8,10},{9,11},{10,12},{11,13},... | collective-permute-start | bytes 786440 | tf_op jit(solution)/shard_map/ppermute | solution.py:268
  11.4 12.7 %collective-permute-start.5 = (bf16[8,128,128]{2,1,0:T(8,128)(2,1)S(1)}, bf16[8,128,128]{2,1,0:T(8,128)(2,1)S(1)}, u32[]{:S(2)}, u32[]{:S(2)}) collective-permute-start(bf16[8,128,128]{2,1,0:T(8,128)(2,1)S(1)} %get-tuple-element.29), channel_id=1, source_target_pairs={{0,4},{1,5},{2,6},{3,7},{8,12},{9,13},{10,14},{11,15},{16,20},{17,... | collective-permute-start | bytes 786440 | tf_op jit(solution)/shard_map/ppermute | solution.py:268
  13.5 12.6 %collective-permute-start.6 = (bf16[8,128,128]{2,1,0:T(8,128)(2,1)S(1)}, bf16[8,128,128]{2,1,0:T(8,128)(2,1)S(1)}, u32[]{:S(2)}, u32[]{:S(2)}) collective-permute-start(bf16[8,128,128]{2,1,0:T(8,128)(2,1)S(1)} %get-tuple-element.31), channel_id=1, source_target_pairs={{4,2},{5,3},{12,10},{13,11},{20,18},{21,19},{28,26},{29,27}} | collective-permute-start | bytes 786440 | tf_op jit(solution)/shard_map/ppermute | solution.py:268
  18.7 12.4 %collective-permute-start.8 = (bf16[8,128,128]{2,1,0:T(8,128)(2,1)S(1)}, bf16[8,128,128]{2,1,0:T(8,128)(2,1)S(1)}, u32[]{:S(2)}, u32[]{:S(2)}) collective-permute-start(bf16[8,128,128]{2,1,0:T(8,128)(2,1)S(1)} %get-tuple-element.35), channel_id=1, source_target_pairs={{2,0},{3,1},{6,4},{7,5},{10,8},{11,9},{14,12},{15,13},{18,16},{19,... | collective-permute-start | bytes 786440 | tf_op jit(solution)/shard_map/ppermute | solution.py:268
  24.8 11.2 %collective-permute-start.9 = (bf16[8,128,128]{2,1,0:T(8,128)(2,1)S(1)}, bf16[8,128,128]{2,1,0:T(8,128)(2,1)S(1)}, u32[]{:S(2)}, u32[]{:S(2)}) collective-permute-start(bf16[8,128,128]{2,1,0:T(8,128)(2,1)S(1)} %get-tuple-element.36), channel_id=1, source_target_pairs={{4,0},{5,1},{6,2},{7,3},{12,8},{13,9},{14,10},{15,11},{20,16},{21,... | collective-permute-start | bytes 786440 | tf_op jit(solution)/shard_map/ppermute | solution.py:268
  29.1 7.0 %collective-permute-start.7 = (bf16[128,32,128]{2,1,0:T(8,128)(2,1)S(1)}, bf16[128,32,128]{2,1,0:T(8,128)(2,1)S(1)}, u32[]{:S(2)}, u32[]{:S(2)}) collective-permute-start(bf16[128,32,128]{2,1,0:T(8,128)(2,1)S(1)} %get-tuple-element.33), channel_id=1, source_target_pairs={{0,1},{1,0},{2,3},{3,2},{4,5},{5,4},{6,7},{7,6},{8,9},{9,8},{10,11... | collective-permute-start | bytes 3145736 | tf_op jit(solution)/shard_map/ppermute | solution.py:264
where the time goes:
time: 37.9 us; the launch traced here: 37.6 us
  Pallas kernels  16.4 us (43%)
  waiting for transfers between devices  10.4 us (27%)
  starting transfers between devices  9.82 us (26%)
  between operations  0.81 us (2%)
    pallas_call x10, Pallas kernels, call(): pl.pallas_call(run, in_specs=(specs or [VMEM] * count) + [VMEM] * len(aft...  16.4 us
    ppermute x5, waiting for transfers between devices, move(): lax.ppermute(value, 'seq', [one for one in pairs if parity in (None, one[...  10.4 us
    ppermute x5, starting transfers between devices, move(): lax.ppermute(value, 'seq', [one for one in pairs if parity in (None, one[...  8.67 us
    ppermute x5, starting transfers between devices, flip(): return lax.ppermute(value, 'seq', [(i, i ^ 1) for i in range(count)])  1.15 us
  transfers between devices with their start and end apart: 10, of which 4 were waited for; matrix products, arithmetic and copies ran while one was open for 0% of the time, Pallas kernels for 40%

commit v1 on v0

--- a/solution.py
+++ b/solution.py
@@ -64,12 +64,15 @@
 
 
 def pack_kernel(k_hbm, v_hbm, all_ref, k_ref, v_ref, sems):
-    copies = start_copies(((k_hbm, k_ref), (v_hbm, v_ref)), sems)
-    kv_count = k_ref.shape[1]
-    for i, ref in enumerate((k_ref, v_ref)):
-        copies[i].wait()
+    rows, kv_count = k_ref.shape[:2]
+    parts = [pl.ds(at, rows // 2) for at in (0, rows // 2)]
+    pairs = [(one.at[part], two.at[part]) for part in parts for one, two in ((k_hbm, k_ref), (v_hbm, v_ref))]
+    copies = start_copies(pairs, sems)
+    for n, copy in enumerate(copies):
+        copy.wait()
+        part, ref = parts[n // 2], (k_ref, v_ref)[n % 2]
         for kv in range(kv_count):
-            all_ref[i * kv_count + kv] = ref[:, kv, :]
+            all_ref[n % 2 * kv_count + kv, part] = ref[part, kv, :]
 
 
 def prep_kernel(q_hbm, g_hbm, o_hbm, log_hbm, q1_ref, g1_ref, o1_ref, log1_ref, *refs):
@@ -274,7 +277,7 @@
         [(full, BF)],
         (hbm(keys), hbm(values)),
         specs=[HBM] * 2,
-        scratch=[pltpu.VMEM(keys.shape, BF)] * 2 + [pltpu.SemaphoreType.DMA((2,))],
+        scratch=[pltpu.VMEM(keys.shape, BF)] * 2 + [pltpu.SemaphoreType.DMA((4,))],
     )
     mid = move(near, 2)
     own = (queries, out_grad, attn_out, log_sums)

time: 37.9 us -> 39.6 us (1.045)
  waiting for transfers between devices: 10.4 us -> 13.7 us
  Pallas kernels: 16.4 us -> 14.7 us
    ppermute x5, waiting for transfers between devices: 10.4 us -> 13.7 us  [move(): lax.ppermute(value, 'seq', [one for one in pairs if parity in (None, one[...]
    pallas_call x10, Pallas kernels: 16.4 us -> 14.7 us  [call(): pl.pallas_call(run, in_specs=(specs or [VMEM] * count) + [VMEM] * len(aft...]
  transfers between devices with their start and end apart: 10 -> 10, of which waited for: 4 -> 4; matrix products, arithmetic and copies ran while one was open for 0% -> 0% of each run, Pallas kernels for 40% -> 34%
where the time goes in v1:
time: 39.6 us; the launch traced here: 39.1 us
  Pallas kernels  14.7 us (37%)
  waiting for transfers between devices  13.7 us (35%)
  starting transfers between devices  9.82 us (25%)
  between operations  0.81 us (2%)
    pallas_call x10, Pallas kernels, call(): pl.pallas_call(run, in_specs=(specs or [VMEM] * count) + [VMEM] * len(aft...  14.7 us
    ppermute x5, waiting for transfers between devices, move(): lax.ppermute(value, 'seq', [one for one in pairs if parity in (None, one[...  13.7 us
    ppermute x5, starting transfers between devices, move(): lax.ppermute(value, 'seq', [one for one in pairs if parity in (None, one[...  8.67 us
    ppermute x5, starting transfers between devices, flip(): return lax.ppermute(value, 'seq', [(i, i ^ 1) for i in range(count)])  1.15 us
  transfers between devices with their start and end apart: 10, of which 4 were waited for; matrix products, arithmetic and copies ran while one was open for 0% of the time, Pallas kernels for 34%

profile of v1, /device:TPU:10, one launch (start us, length us, event | category | flops | bytes accessed | tf_op | source)
XLA Modules:
  0.0 39.1 jit_solution(1281611063699453238)
XLA Ops:
  0.6 0.1 collective-permute-start
  0.7 0.5 %collective-permute-start.1 = (bf16[128,32,128]{2,1,0:T(8,128)(2,1)}, bf16[128,32,128]{2,1,0:T(8,128)(2,1)S(1)}, u32[]{:S(2)}, u32[]{:S(2)}) collective-permute-start(bf16[128,32,128]{2,1,0:T(8,128)(2,1)} %refs_2_.3), channel_id=1, source_target_pairs={{0,1},{1,0},{2,3},{3,2},{4,5},{5,4},{6,7},{7,6},{8,9},{9,8},{10,11... | collective-permute-start | bytes 3145736 | tf_op jit(solution)/shard_map/ppermute | solution.py:267
  1.2 0.1 collective-permute-start.2
  1.3 0.4 %collective-permute-start.3 = (f32[32,128]{1,0:T(8,128)}, f32[32,128]{1,0:T(8,128)S(1)}, u32[]{:S(2)}, u32[]{:S(2)}) collective-permute-start(f32[32,128]{1,0:T(8,128)} %refs_4_.1), channel_id=1, source_target_pairs={{0,1},{1,0},{2,3},{3,2},{4,5},{5,4},{6,7},{7,6},{8,9},{9,8},{10,11... | collective-permute-start | bytes 49160 | tf_op jit(solution)/shard_map/ppermute | solution.py:267
  1.7 1.4 %pack.1.refs_3_ = bf16[8,128,128]{2,1,0:T(8,128)(2,1)S(1)} custom-call(bf16[128,4,128]{2,1,0:T(4,128)(2,1)} %refs_0_.3, bf16[128,4,128]{2,1,0:T(4,128)(2,1)} %refs_1_.5), custom_call_target="tpu_custom_call" | custom-call | flops 10000000000 | bytes 10000000 | tf_op jit(solution)/shard_map/pack/pallas_call | solution.py:38
  3.1 0.0 copy-start
  3.1 3.5 %collective-permute-start.4 = (bf16[8,128,128]{2,1,0:T(8,128)(2,1)S(1)}, bf16[8,128,128]{2,1,0:T(8,128)(2,1)S(1)}, u32[]{:S(2)}, u32[]{:S(2)}) collective-permute-start(bf16[8,128,128]{2,1,0:T(8,128)(2,1)S(1)} %pack.1.refs_3_), channel_id=1, source_target_pairs={{0,2},{1,3},{2,4},{3,5},{4,6},{5,7},{8,10},{9,11},{10,12},{11,13},... | collective-permute-start | bytes 786440 | tf_op jit(solution)/shard_map/ppermute | solution.py:271
  6.6 0.0 collective-permute-done.3.refs_7_.refs_8_
  6.6 0.0 collective-permute-done.refs_4_.refs_5_
  6.6 0.0 collective-permute-done.1.refs_5_.refs_6_
  6.6 0.0 collective-permute-done.2.refs_6_.refs_7_
  6.6 2.8 %prep_early.1 = (bf16[2,2,4,1024,128]{4,3,2,1,0:T(8,128)(2,1)S(1)}, f32[2,2,4,1024,128]{4,3,2,1,0:T(8,128)S(1)}) custom-call(bf16[128,32,128]{2,1,0:T(8,128)(2,1)} %refs_1_.4, bf16[128,32,128]{2,1,0:T(8,128)(2,1)} %refs_2_.3, bf16[128,32,128]{2,1,0:T(8,128)(2,1)} %refs_3_.3, f32[32,128]{1,0:T(8,128)} %refs_4_.1, ...), custom_call_target="tpu_custom_call" | custom-call | flops 10000000000 | bytes 10000000 | tf_op jit(solution)/shard_map/prep_early/pallas_call | solution.py:38
  9.5 0.0 copy-done
  9.5 1.7 %near_early.1 = (bf16[8,128,128]{2,1,0:T(8,128)(2,1)S(1)}, bf16[2,4,1024,128]{3,2,1,0:T(8,128)(2,1)S(1)}, f32[8,128,128]{2,1,0:T(8,128)S(1)}) custom-call(s32[8,128]{1,0:T(8,128)S(1)} %bitcast.1, bf16[2,2,4,1024,128]{4,3,2,1,0:T(8,128)(2,1)S(1)} %get-tuple-element.20.refs_9_.refs_1_, f32[2,2,4,1024,128]{4,3,2,1,0:T(8,128)S(1)} %get-tuple-element.21.refs_10_.refs_2_, ...), custom_call_target="tpu_custom_call" | custom-call | flops 10000000000 | bytes 10000000 | tf_op jit(solution)/shard_map/near_early/pallas_call | solution.py:38
  11.2 1.3 %collective-permute-start.5 = (bf16[8,128,128]{2,1,0:T(8,128)(2,1)S(1)}, bf16[8,128,128]{2,1,0:T(8,128)(2,1)S(1)}, u32[]{:S(2)}, u32[]{:S(2)}) collective-permute-start(bf16[8,128,128]{2,1,0:T(8,128)(2,1)S(1)} %get-tuple-element.29), channel_id=1, source_target_pairs={{0,4},{1,5},{2,6},{3,7},{8,12},{9,13},{10,14},{11,15},{16,20},{17,... | collective-permute-start | bytes 786440 | tf_op jit(solution)/shard_map/ppermute | solution.py:271
  12.5 0.3 prep_late.1
  12.8 0.5 %collective-permute-done.4.refs_3_.refs_8_.refs_4_ = bf16[8,128,128]{2,1,0:T(8,128)(2,1)S(1)} collective-permute-done((bf16[8,128,128]{2,1,0:T(8,128)(2,1)S(1)}, bf16[8,128,128]{2,1,0:T(8,128)(2,1)S(1)}, u32[]{:S(2)}, u32[]{:S(2)}) %collective-permute-start.4) | collective-permute-done | bytes 262176 | tf_op jit(solution)/shard_map/ppermute | solution.py:271
  13.3 1.3 %collective-permute-start.6 = (bf16[8,128,128]{2,1,0:T(8,128)(2,1)S(1)}, bf16[8,128,128]{2,1,0:T(8,128)(2,1)S(1)}, u32[]{:S(2)}, u32[]{:S(2)}) collective-permute-start(bf16[8,128,128]{2,1,0:T(8,128)(2,1)S(1)} %get-tuple-element.31), channel_id=1, source_target_pairs={{4,2},{5,3},{12,10},{13,11},{20,18},{21,19},{28,26},{29,27}} | collective-permute-start | bytes 786440 | tf_op jit(solution)/shard_map/ppermute | solution.py:271
  14.6 2.4 %mid_odd.1 = (bf16[2,4,1024,128]{3,2,1,0:T(8,128)(2,1)S(1)}, bf16[8,128,128]{2,1,0:T(8,128)(2,1)S(1)}) custom-call(s32[8,128]{1,0:T(8,128)S(1)} %get-tuple-element.22.refs_0_, bf16[2,2,4,1024,128]{4,3,2,1,0:T(8,128)(2,1)S(1)} %get-tuple-element.23.refs_1_, f32[2,2,4,1024,128]{4,3,2,1,0:T(8,128)S(1)} %get-tuple-element.24.refs_2_, ...), custom_call_target="tpu_custom_call", output_to_operand_aliasing={{0}: (4, {})} | custom-call | flops 10000000000 | bytes 10000000 | tf_op jit(solution)/shard_map/mid_odd/pallas_call | solution.py:38
  17.0 1.3 %collective-permute-start.8 = (bf16[8,128,128]{2,1,0:T(8,128)(2,1)S(1)}, bf16[8,128,128]{2,1,0:T(8,128)(2,1)S(1)}, u32[]{:S(2)}, u32[]{:S(2)}) collective-permute-start(bf16[8,128,128]{2,1,0:T(8,128)(2,1)S(1)} %get-tuple-element.35), channel_id=1, source_target_pairs={{2,0},{3,1},{6,4},{7,5},{10,8},{11,9},{14,12},{15,13},{18,16},{19,... | collective-permute-start | bytes 786440 | tf_op jit(solution)/shard_map/ppermute | solution.py:271
  18.3 5.9 %collective-permute-done.5.refs_3_.refs_9_.refs_5_ = bf16[8,128,128]{2,1,0:T(8,128)(2,1)S(1)} collective-permute-done((bf16[8,128,128]{2,1,0:T(8,128)(2,1)S(1)}, bf16[8,128,128]{2,1,0:T(8,128)(2,1)S(1)}, u32[]{:S(2)}, u32[]{:S(2)}) %collective-permute-start.5) | collective-permute-done | bytes 262176 | tf_op jit(solution)/shard_map/ppermute | solution.py:271
  24.1 0.7 %far.1 = (bf16[2,4,1024,128]{3,2,1,0:T(8,128)(2,1)S(1)}, bf16[8,128,128]{2,1,0:T(8,128)(2,1)S(1)}) custom-call(s32[8,128]{1,0:T(8,128)S(1)} %get-tuple-element.22.refs_0_, bf16[2,2,4,1024,128]{4,3,2,1,0:T(8,128)(2,1)S(1)} %get-tuple-element.23.refs_1_, f32[2,2,4,1024,128]{4,3,2,1,0:T(8,128)S(1)} %get-tuple-element.24.refs_2_, ...), custom_call_target="tpu_custom_call" | custom-call | flops 10000000000 | bytes 10000000 | tf_op jit(solution)/shard_map/far/pallas_call | solution.py:38
  24.8 1.3 %collective-permute-start.9 = (bf16[8,128,128]{2,1,0:T(8,128)(2,1)S(1)}, bf16[8,128,128]{2,1,0:T(8,128)(2,1)S(1)}, u32[]{:S(2)}, u32[]{:S(2)}) collective-permute-start(bf16[8,128,128]{2,1,0:T(8,128)(2,1)S(1)} %get-tuple-element.36), channel_id=1, source_target_pairs={{4,0},{5,1},{6,2},{7,3},{12,8},{13,9},{14,10},{15,11},{20,16},{21,... | collective-permute-start | bytes 786440 | tf_op jit(solution)/shard_map/ppermute | solution.py:271
  26.1 0.9 %collective-permute-done.6.refs_10_ = bf16[8,128,128]{2,1,0:T(8,128)(2,1)S(1)} collective-permute-done((bf16[8,128,128]{2,1,0:T(8,128)(2,1)S(1)}, bf16[8,128,128]{2,1,0:T(8,128)(2,1)S(1)}, u32[]{:S(2)}, u32[]{:S(2)}) %collective-permute-start.6) | collective-permute-done | bytes 262176 | tf_op jit(solution)/shard_map/ppermute | solution.py:271
  27.1 2.9 %near.1 = (bf16[2,4,1024,128]{3,2,1,0:T(8,128)(2,1)S(1)}, f32[8,128,128]{2,1,0:T(8,128)S(1)}, bf16[128,32,128]{2,1,0:T(8,128)(2,1)S(1)}) custom-call(s32[8,128]{1,0:T(8,128)S(1)} %get-tuple-element.22.refs_0_, bf16[2,2,4,1024,128]{4,3,2,1,0:T(8,128)(2,1)S(1)} %get-tuple-element.23.refs_1_, ...), custom_call_target="tpu_custom_call", output_to_operand_aliasing={{0}: (4, {})} | custom-call | flops 10000000000 | bytes 10000000 | tf_op jit(solution)/shard_map/near/pallas_call | solution.py:38
  30.0 0.1 collective-permute-start.7
  30.1 1.0 %query_own.1.refs_0_ = f32[128,32,128]{2,1,0:T(8,128)S(1)} custom-call(bf16[2,4,1024,128]{3,2,1,0:T(8,128)(2,1)S(1)} %get-tuple-element.32.refs_0_, bf16[2,4,1024,128]{3,2,1,0:T(8,128)(2,1)S(1)} %get-tuple-element.28.refs_4_.refs_6_.refs_1_, bf16[2,4,1024,128]{3,2,1,0:T(8,128)(2,1)S(1)} %get-tuple-element.30.refs_7_.refs_2_, ...), custom_call_target="tpu_custom_call" | custom-call | flops 10000000000 | bytes 10000000 | tf_op jit(solution)/shard_map/query_own/pallas_call | solution.py:38
  31.1 0.0 collective-permute-done.8
  31.1 6.4 %collective-permute-done.9 = bf16[8,128,128]{2,1,0:T(8,128)(2,1)S(1)} collective-permute-done((bf16[8,128,128]{2,1,0:T(8,128)(2,1)S(1)}, bf16[8,128,128]{2,1,0:T(8,128)(2,1)S(1)}, u32[]{:S(2)}, u32[]{:S(2)}) %collective-permute-start.9) | collective-permute-done | bytes 262176 | tf_op jit(solution)/shard_map/ppermute | solution.py:271
  37.5 0.1 convert_add_fusion.refs_2_
  37.6 0.0 collective-permute-done.7.refs_1_
  37.6 1.5 %sums.1 = (bf16[128,32,128]{2,1,0:T(8,128)(2,1)}, bf16[128,4,128]{2,1,0:T(4,128)(2,1)}, bf16[128,4,128]{2,1,0:T(4,128)(2,1)}) custom-call(f32[128,32,128]{2,1,0:T(8,128)S(1)} %query_own.1.refs_0_, bf16[128,32,128]{2,1,0:T(8,128)(2,1)S(1)} %collective-permute-done.7.refs_1_, f32[8,128,128]{2,1,0:T(8,128)S(1)} %convert_add_fusion.refs_2_), custom_call_target="tpu_custom_call" | custom-call | flops 10000000000 | bytes 10000000 | tf_op jit(solution)/shard_map/sums/pallas_call | solution.py:38
  (1 shorter events, 0.0 us)
Async XLA Ops:
  0.6 6.0 %collective-permute-start = (bf16[128,32,128]{2,1,0:T(8,128)(2,1)}, bf16[128,32,128]{2,1,0:T(8,128)(2,1)S(1)}, u32[]{:S(2)}, u32[]{:S(2)}) collective-permute-start(bf16[128,32,128]{2,1,0:T(8,128)(2,1)} %refs_1_.4), channel_id=1, source_target_pairs={{0,1},{1,0},{2,3},{3,2},{4,5},{5,4},{6,7},{7,6},{8,9},{9,8},{10,11... | collective-permute-start | bytes 3145736 | tf_op jit(solution)/shard_map/ppermute | solution.py:267
  0.7 5.9 %collective-permute-start.1 = (bf16[128,32,128]{2,1,0:T(8,128)(2,1)}, bf16[128,32,128]{2,1,0:T(8,128)(2,1)S(1)}, u32[]{:S(2)}, u32[]{:S(2)}) collective-permute-start(bf16[128,32,128]{2,1,0:T(8,128)(2,1)} %refs_2_.3), channel_id=1, source_target_pairs={{0,1},{1,0},{2,3},{3,2},{4,5},{5,4},{6,7},{7,6},{8,9},{9,8},{10,11... | collective-permute-start | bytes 3145736 | tf_op jit(solution)/shard_map/ppermute | solution.py:267
  1.2 5.4 %collective-permute-start.2 = (bf16[128,32,128]{2,1,0:T(8,128)(2,1)}, bf16[128,32,128]{2,1,0:T(8,128)(2,1)S(1)}, u32[]{:S(2)}, u32[]{:S(2)}) collective-permute-start(bf16[128,32,128]{2,1,0:T(8,128)(2,1)} %refs_3_.3), channel_id=1, source_target_pairs={{0,1},{1,0},{2,3},{3,2},{4,5},{5,4},{6,7},{7,6},{8,9},{9,8},{10,11... | collective-permute-start | bytes 3145736 | tf_op jit(solution)/shard_map/ppermute | solution.py:267
  1.3 5.3 %collective-permute-start.3 = (f32[32,128]{1,0:T(8,128)}, f32[32,128]{1,0:T(8,128)S(1)}, u32[]{:S(2)}, u32[]{:S(2)}) collective-permute-start(f32[32,128]{1,0:T(8,128)} %refs_4_.1), channel_id=1, source_target_pairs={{0,1},{1,0},{2,3},{3,2},{4,5},{5,4},{6,7},{7,6},{8,9},{9,8},{10,11... | collective-permute-start | bytes 49160 | tf_op jit(solution)/shard_map/ppermute | solution.py:267
  3.1 6.4 %copy-start = (s32[1024]{0:T(1024)S(1)}, s32[1024]{0:T(1024)}, u32[]{:S(2)}) copy-start(s32[1024]{0:T(1024)} %param.13) | copy-start | bytes 12292
  3.1 10.2 %collective-permute-start.4 = (bf16[8,128,128]{2,1,0:T(8,128)(2,1)S(1)}, bf16[8,128,128]{2,1,0:T(8,128)(2,1)S(1)}, u32[]{:S(2)}, u32[]{:S(2)}) collective-permute-start(bf16[8,128,128]{2,1,0:T(8,128)(2,1)S(1)} %pack.1.refs_3_), channel_id=1, source_target_pairs={{0,2},{1,3},{2,4},{3,5},{4,6},{5,7},{8,10},{9,11},{10,12},{11,13},... | collective-permute-start | bytes 786440 | tf_op jit(solution)/shard_map/ppermute | solution.py:271
  11.2 12.9 %collective-permute-start.5 = (bf16[8,128,128]{2,1,0:T(8,128)(2,1)S(1)}, bf16[8,128,128]{2,1,0:T(8,128)(2,1)S(1)}, u32[]{:S(2)}, u32[]{:S(2)}) collective-permute-start(bf16[8,128,128]{2,1,0:T(8,128)(2,1)S(1)} %get-tuple-element.29), channel_id=1, source_target_pairs={{0,4},{1,5},{2,6},{3,7},{8,12},{9,13},{10,14},{11,15},{16,20},{17,... | collective-permute-start | bytes 786440 | tf_op jit(solution)/shard_map/ppermute | solution.py:271
  13.3 13.8 %collective-permute-start.6 = (bf16[8,128,128]{2,1,0:T(8,128)(2,1)S(1)}, bf16[8,128,128]{2,1,0:T(8,128)(2,1)S(1)}, u32[]{:S(2)}, u32[]{:S(2)}) collective-permute-start(bf16[8,128,128]{2,1,0:T(8,128)(2,1)S(1)} %get-tuple-element.31), channel_id=1, source_target_pairs={{4,2},{5,3},{12,10},{13,11},{20,18},{21,19},{28,26},{29,27}} | collective-permute-start | bytes 786440 | tf_op jit(solution)/shard_map/ppermute | solution.py:271
  17.0 14.1 %collective-permute-start.8 = (bf16[8,128,128]{2,1,0:T(8,128)(2,1)S(1)}, bf16[8,128,128]{2,1,0:T(8,128)(2,1)S(1)}, u32[]{:S(2)}, u32[]{:S(2)}) collective-permute-start(bf16[8,128,128]{2,1,0:T(8,128)(2,1)S(1)} %get-tuple-element.35), channel_id=1, source_target_pairs={{2,0},{3,1},{6,4},{7,5},{10,8},{11,9},{14,12},{15,13},{18,16},{19,... | collective-permute-start | bytes 786440 | tf_op jit(solution)/shard_map/ppermute | solution.py:271
  24.8 12.7 %collective-permute-start.9 = (bf16[8,128,128]{2,1,0:T(8,128)(2,1)S(1)}, bf16[8,128,128]{2,1,0:T(8,128)(2,1)S(1)}, u32[]{:S(2)}, u32[]{:S(2)}) collective-permute-start(bf16[8,128,128]{2,1,0:T(8,128)(2,1)S(1)} %get-tuple-element.36), channel_id=1, source_target_pairs={{4,0},{5,1},{6,2},{7,3},{12,8},{13,9},{14,10},{15,11},{20,16},{21,... | collective-permute-start | bytes 786440 | tf_op jit(solution)/shard_map/ppermute | solution.py:271
  30.0 7.6 %collective-permute-start.7 = (bf16[128,32,128]{2,1,0:T(8,128)(2,1)S(1)}, bf16[128,32,128]{2,1,0:T(8,128)(2,1)S(1)}, u32[]{:S(2)}, u32[]{:S(2)}) collective-permute-start(bf16[128,32,128]{2,1,0:T(8,128)(2,1)S(1)} %get-tuple-element.33), channel_id=1, source_target_pairs={{0,1},{1,0},{2,3},{3,2},{4,5},{5,4},{6,7},{7,6},{8,9},{9,8},{10,11... | collective-permute-start | bytes 3145736 | tf_op jit(solution)/shard_map/ppermute | solution.py:267

commit v2 on v0

--- a/solution.py
+++ b/solution.py
@@ -248,8 +248,8 @@
     query_ref[...] = (one_ref[...] + two_ref[...].astype(F32)).astype(BF)
     kv_count = key_ref.shape[1]
     for i, ref in enumerate((key_ref, val_ref)):
-        heads = [sums_ref[i * kv_count + kv] for kv in range(kv_count)]
-        ref[...] = jnp.stack(heads, axis=1).astype(BF)
+        heads = [sums_ref[i * kv_count + kv].astype(BF) for kv in range(kv_count)]
+        ref[...] = jnp.stack(heads, axis=1)
 
 
 def on_device(queries, keys, values, attn_out, out_grad, log_sums, doc_ids):

time: 37.9 us -> 40.4 us (1.066)
  the two profiles are of different devices: /device:TPU:10 before, /device:TPU:5 now
where the time goes in v2:
time: 40.4 us; the launch traced here: 39.7 us
  waiting for transfers between devices  14.9 us (37%)
  Pallas kernels  12 us (30%)
  starting transfers between devices  11.8 us (29%)
  between operations  0.79 us (2%)
    ppermute x5, waiting for transfers between devices, move(): lax.ppermute(value, 'seq', [one for one in pairs if parity in (None, one[...  14.8 us
    pallas_call x10, Pallas kernels, call(): pl.pallas_call(run, in_specs=(specs or [VMEM] * count) + [VMEM] * len(aft...  12 us
    ppermute x5, starting transfers between devices, move(): lax.ppermute(value, 'seq', [one for one in pairs if parity in (None, one[...  7.78 us
    ppermute x5, starting transfers between devices, flip(): return lax.ppermute(value, 'seq', [(i, i ^ 1) for i in range(count)])  4.06 us
  transfers between devices with their start and end apart: 10, of which 4 were waited for; matrix products, arithmetic and copies ran while one was open for 0% of the time, Pallas kernels for 26%

profile of v2, /device:TPU:5, one launch (start us, length us, event | category | flops | bytes accessed | tf_op | source)
XLA Modules:
  0.0 39.7 jit_solution(14687420380855364397)
XLA Ops:
  0.6 0.7 %collective-permute-start = (bf16[128,32,128]{2,1,0:T(8,128)(2,1)}, bf16[128,32,128]{2,1,0:T(8,128)(2,1)S(1)}, u32[]{:S(2)}, u32[]{:S(2)}) collective-permute-start(bf16[128,32,128]{2,1,0:T(8,128)(2,1)} %refs_1_.4), channel_id=1, source_target_pairs={{0,1},{1,0},{2,3},{3,2},{4,5},{5,4},{6,7},{7,6},{8,9},{9,8},{10,11... | collective-permute-start | bytes 3145736 | tf_op jit(solution)/shard_map/ppermute | solution.py:264
  1.4 0.1 collective-permute-start.1
  1.5 0.4 %collective-permute-start.2 = (bf16[128,32,128]{2,1,0:T(8,128)(2,1)}, bf16[128,32,128]{2,1,0:T(8,128)(2,1)S(1)}, u32[]{:S(2)}, u32[]{:S(2)}) collective-permute-start(bf16[128,32,128]{2,1,0:T(8,128)(2,1)} %refs_3_.3), channel_id=1, source_target_pairs={{0,1},{1,0},{2,3},{3,2},{4,5},{5,4},{6,7},{7,6},{8,9},{9,8},{10,11... | collective-permute-start | bytes 3145736 | tf_op jit(solution)/shard_map/ppermute | solution.py:264
  1.9 0.1 collective-permute-start.3
  2.0 1.5 %pack.1.refs_3_ = bf16[8,128,128]{2,1,0:T(8,128)(2,1)S(1)} custom-call(bf16[128,4,128]{2,1,0:T(4,128)(2,1)} %refs_0_.3, bf16[128,4,128]{2,1,0:T(4,128)(2,1)} %refs_1_.5), custom_call_target="tpu_custom_call" | custom-call | flops 10000000000 | bytes 10000000 | tf_op jit(solution)/shard_map/pack/pallas_call | solution.py:38
  3.5 0.0 copy-start
  3.5 3.2 %collective-permute-start.4 = (bf16[8,128,128]{2,1,0:T(8,128)(2,1)S(1)}, bf16[8,128,128]{2,1,0:T(8,128)(2,1)S(1)}, u32[]{:S(2)}, u32[]{:S(2)}) collective-permute-start(bf16[8,128,128]{2,1,0:T(8,128)(2,1)S(1)} %pack.1.refs_3_), channel_id=1, source_target_pairs={{0,2},{1,3},{2,4},{3,5},{4,6},{5,7},{8,10},{9,11},{10,12},{11,13},... | collective-permute-start | bytes 786440 | tf_op jit(solution)/shard_map/ppermute | solution.py:268
  6.7 0.1 collective-permute-done.3.refs_7_.refs_8_
  6.9 0.0 collective-permute-done.refs_4_.refs_5_
  6.9 0.0 collective-permute-done.1.refs_5_.refs_6_
  6.9 0.0 collective-permute-done.2.refs_6_.refs_7_
  6.9 2.8 %prep_early.1 = (bf16[2,2,4,1024,128]{4,3,2,1,0:T(8,128)(2,1)S(1)}, f32[2,2,4,1024,128]{4,3,2,1,0:T(8,128)S(1)}) custom-call(bf16[128,32,128]{2,1,0:T(8,128)(2,1)} %refs_1_.4, bf16[128,32,128]{2,1,0:T(8,128)(2,1)} %refs_2_.3, bf16[128,32,128]{2,1,0:T(8,128)(2,1)} %refs_3_.3, f32[32,128]{1,0:T(8,128)} %refs_4_.1, ...), custom_call_target="tpu_custom_call" | custom-call | flops 10000000000 | bytes 10000000 | tf_op jit(solution)/shard_map/prep_early/pallas_call | solution.py:38
  9.8 0.0 copy-done
  9.8 1.7 %near_early.1 = (bf16[8,128,128]{2,1,0:T(8,128)(2,1)S(1)}, bf16[2,4,1024,128]{3,2,1,0:T(8,128)(2,1)S(1)}, f32[8,128,128]{2,1,0:T(8,128)S(1)}) custom-call(s32[8,128]{1,0:T(8,128)S(1)} %bitcast.1, bf16[2,2,4,1024,128]{4,3,2,1,0:T(8,128)(2,1)S(1)} %get-tuple-element.20.refs_9_.refs_1_, f32[2,2,4,1024,128]{4,3,2,1,0:T(8,128)S(1)} %get-tuple-element.21.refs_10_.refs_2_, ...), custom_call_target="tpu_custom_call" | custom-call | flops 10000000000 | bytes 10000000 | tf_op jit(solution)/shard_map/near_early/pallas_call | solution.py:38
  11.5 1.3 %collective-permute-start.5 = (bf16[8,128,128]{2,1,0:T(8,128)(2,1)S(1)}, bf16[8,128,128]{2,1,0:T(8,128)(2,1)S(1)}, u32[]{:S(2)}, u32[]{:S(2)}) collective-permute-start(bf16[8,128,128]{2,1,0:T(8,128)(2,1)S(1)} %get-tuple-element.29), channel_id=1, source_target_pairs={{0,4},{1,5},{2,6},{3,7},{8,12},{9,13},{10,14},{11,15},{16,20},{17,... | collective-permute-start | bytes 786440 | tf_op jit(solution)/shard_map/ppermute | solution.py:268
  12.8 0.3 prep_late.1
  13.1 0.0 collective-permute-done.4.refs_3_.refs_8_.refs_4_
  13.1 0.7 %mid_even.1 = (bf16[2,4,1024,128]{3,2,1,0:T(8,128)(2,1)S(1)}, bf16[8,128,128]{2,1,0:T(8,128)(2,1)S(1)}) custom-call(s32[8,128]{1,0:T(8,128)S(1)} %get-tuple-element.22.refs_0_, bf16[2,2,4,1024,128]{4,3,2,1,0:T(8,128)(2,1)S(1)} %get-tuple-element.23.refs_1_, f32[2,2,4,1024,128]{4,3,2,1,0:T(8,128)S(1)} %get-tuple-element.24.refs_2_, ...), custom_call_target="tpu_custom_call" | custom-call | flops 10000000000 | bytes 10000000 | tf_op jit(solution)/shard_map/mid_even/pallas_call | solution.py:38
  13.8 0.7 %collective-permute-start.6 = (bf16[8,128,128]{2,1,0:T(8,128)(2,1)S(1)}, bf16[8,128,128]{2,1,0:T(8,128)(2,1)S(1)}, u32[]{:S(2)}, u32[]{:S(2)}) collective-permute-start(bf16[8,128,128]{2,1,0:T(8,128)(2,1)S(1)} %get-tuple-element.31), channel_id=1, source_target_pairs={{4,2},{5,3},{12,10},{13,11},{20,18},{21,19},{28,26},{29,27}} | collective-permute-start | bytes 786440 | tf_op jit(solution)/shard_map/ppermute | solution.py:268
  14.5 0.2 mid_odd.1
  14.7 1.3 %collective-permute-start.8 = (bf16[8,128,128]{2,1,0:T(8,128)(2,1)S(1)}, bf16[8,128,128]{2,1,0:T(8,128)(2,1)S(1)}, u32[]{:S(2)}, u32[]{:S(2)}) collective-permute-start(bf16[8,128,128]{2,1,0:T(8,128)(2,1)S(1)} %get-tuple-element.35), channel_id=1, source_target_pairs={{2,0},{3,1},{6,4},{7,5},{10,8},{11,9},{14,12},{15,13},{18,16},{19,... | collective-permute-start | bytes 786440 | tf_op jit(solution)/shard_map/ppermute | solution.py:268
  16.0 2.1 %collective-permute-done.5.refs_3_.refs_9_.refs_5_ = bf16[8,128,128]{2,1,0:T(8,128)(2,1)S(1)} collective-permute-done((bf16[8,128,128]{2,1,0:T(8,128)(2,1)S(1)}, bf16[8,128,128]{2,1,0:T(8,128)(2,1)S(1)}, u32[]{:S(2)}, u32[]{:S(2)}) %collective-permute-start.5) | collective-permute-done | bytes 262176 | tf_op jit(solution)/shard_map/ppermute | solution.py:268
  18.2 0.7 %far.1 = (bf16[2,4,1024,128]{3,2,1,0:T(8,128)(2,1)S(1)}, bf16[8,128,128]{2,1,0:T(8,128)(2,1)S(1)}) custom-call(s32[8,128]{1,0:T(8,128)S(1)} %get-tuple-element.22.refs_0_, bf16[2,2,4,1024,128]{4,3,2,1,0:T(8,128)(2,1)S(1)} %get-tuple-element.23.refs_1_, f32[2,2,4,1024,128]{4,3,2,1,0:T(8,128)S(1)} %get-tuple-element.24.refs_2_, ...), custom_call_target="tpu_custom_call" | custom-call | flops 10000000000 | bytes 10000000 | tf_op jit(solution)/shard_map/far/pallas_call | solution.py:38
  18.9 1.3 %collective-permute-start.9 = (bf16[8,128,128]{2,1,0:T(8,128)(2,1)S(1)}, bf16[8,128,128]{2,1,0:T(8,128)(2,1)S(1)}, u32[]{:S(2)}, u32[]{:S(2)}) collective-permute-start(bf16[8,128,128]{2,1,0:T(8,128)(2,1)S(1)} %get-tuple-element.36), channel_id=1, source_target_pairs={{4,0},{5,1},{6,2},{7,3},{12,8},{13,9},{14,10},{15,11},{20,16},{21,... | collective-permute-start | bytes 786440 | tf_op jit(solution)/shard_map/ppermute | solution.py:268
  20.2 0.0 collective-permute-done.6.refs_10_
  20.2 1.4 %near.1 = (bf16[2,4,1024,128]{3,2,1,0:T(8,128)(2,1)S(1)}, f32[8,128,128]{2,1,0:T(8,128)S(1)}, bf16[128,32,128]{2,1,0:T(8,128)(2,1)S(1)}) custom-call(s32[8,128]{1,0:T(8,128)S(1)} %get-tuple-element.22.refs_0_, bf16[2,2,4,1024,128]{4,3,2,1,0:T(8,128)(2,1)S(1)} %get-tuple-element.23.refs_1_, ...), custom_call_target="tpu_custom_call", output_to_operand_aliasing={{0}: (4, {})} | custom-call | flops 10000000000 | bytes 10000000 | tf_op jit(solution)/shard_map/near/pallas_call | solution.py:38
  21.6 2.7 %collective-permute-start.7 = (bf16[128,32,128]{2,1,0:T(8,128)(2,1)S(1)}, bf16[128,32,128]{2,1,0:T(8,128)(2,1)S(1)}, u32[]{:S(2)}, u32[]{:S(2)}) collective-permute-start(bf16[128,32,128]{2,1,0:T(8,128)(2,1)S(1)} %get-tuple-element.33), channel_id=1, source_target_pairs={{0,1},{1,0},{2,3},{3,2},{4,5},{5,4},{6,7},{7,6},{8,9},{9,8},{10,11... | collective-permute-start | bytes 3145736 | tf_op jit(solution)/shard_map/ppermute | solution.py:264
  24.3 1.0 %query_own.1.refs_0_ = f32[128,32,128]{2,1,0:T(8,128)S(1)} custom-call(bf16[2,4,1024,128]{3,2,1,0:T(8,128)(2,1)S(1)} %get-tuple-element.32.refs_0_, bf16[2,4,1024,128]{3,2,1,0:T(8,128)(2,1)S(1)} %get-tuple-element.28.refs_4_.refs_6_.refs_1_, bf16[2,4,1024,128]{3,2,1,0:T(8,128)(2,1)S(1)} %get-tuple-element.30.refs_7_.refs_2_, ...), custom_call_target="tpu_custom_call" | custom-call | flops 10000000000 | bytes 10000000 | tf_op jit(solution)/shard_map/query_own/pallas_call | solution.py:38
  25.3 0.4 collective-permute-done.8
  25.7 12.3 %collective-permute-done.9 = bf16[8,128,128]{2,1,0:T(8,128)(2,1)S(1)} collective-permute-done((bf16[8,128,128]{2,1,0:T(8,128)(2,1)S(1)}, bf16[8,128,128]{2,1,0:T(8,128)(2,1)S(1)}, u32[]{:S(2)}, u32[]{:S(2)}) %collective-permute-start.9) | collective-permute-done | bytes 262176 | tf_op jit(solution)/shard_map/ppermute | solution.py:268
  38.0 0.1 convert_add_fusion.refs_2_
  38.1 0.0 collective-permute-done.7.refs_1_
  38.1 1.6 %sums.1 = (bf16[128,32,128]{2,1,0:T(8,128)(2,1)}, bf16[128,4,128]{2,1,0:T(4,128)(2,1)}, bf16[128,4,128]{2,1,0:T(4,128)(2,1)}) custom-call(f32[128,32,128]{2,1,0:T(8,128)S(1)} %query_own.1.refs_0_, bf16[128,32,128]{2,1,0:T(8,128)(2,1)S(1)} %collective-permute-done.7.refs_1_, f32[8,128,128]{2,1,0:T(8,128)S(1)} %convert_add_fusion.refs_2_), custom_call_target="tpu_custom_call" | custom-call | flops 10000000000 | bytes 10000000 | tf_op jit(solution)/shard_map/sums/pallas_call | solution.py:38
Async XLA Ops:
  0.6 6.3 %collective-permute-start = (bf16[128,32,128]{2,1,0:T(8,128)(2,1)}, bf16[128,32,128]{2,1,0:T(8,128)(2,1)S(1)}, u32[]{:S(2)}, u32[]{:S(2)}) collective-permute-start(bf16[128,32,128]{2,1,0:T(8,128)(2,1)} %refs_1_.4), channel_id=1, source_target_pairs={{0,1},{1,0},{2,3},{3,2},{4,5},{5,4},{6,7},{7,6},{8,9},{9,8},{10,11... | collective-permute-start | bytes 3145736 | tf_op jit(solution)/shard_map/ppermute | solution.py:264
  1.4 5.5 %collective-permute-start.1 = (bf16[128,32,128]{2,1,0:T(8,128)(2,1)}, bf16[128,32,128]{2,1,0:T(8,128)(2,1)S(1)}, u32[]{:S(2)}, u32[]{:S(2)}) collective-permute-start(bf16[128,32,128]{2,1,0:T(8,128)(2,1)} %refs_2_.3), channel_id=1, source_target_pairs={{0,1},{1,0},{2,3},{3,2},{4,5},{5,4},{6,7},{7,6},{8,9},{9,8},{10,11... | collective-permute-start | bytes 3145736 | tf_op jit(solution)/shard_map/ppermute | solution.py:264
  1.5 5.4 %collective-permute-start.2 = (bf16[128,32,128]{2,1,0:T(8,128)(2,1)}, bf16[128,32,128]{2,1,0:T(8,128)(2,1)S(1)}, u32[]{:S(2)}, u32[]{:S(2)}) collective-permute-start(bf16[128,32,128]{2,1,0:T(8,128)(2,1)} %refs_3_.3), channel_id=1, source_target_pairs={{0,1},{1,0},{2,3},{3,2},{4,5},{5,4},{6,7},{7,6},{8,9},{9,8},{10,11... | collective-permute-start | bytes 3145736 | tf_op jit(solution)/shard_map/ppermute | solution.py:264
  1.9 5.0 %collective-permute-start.3 = (f32[32,128]{1,0:T(8,128)}, f32[32,128]{1,0:T(8,128)S(1)}, u32[]{:S(2)}, u32[]{:S(2)}) collective-permute-start(f32[32,128]{1,0:T(8,128)} %refs_4_.1), channel_id=1, source_target_pairs={{0,1},{1,0},{2,3},{3,2},{4,5},{5,4},{6,7},{7,6},{8,9},{9,8},{10,11... | collective-permute-start | bytes 49160 | tf_op jit(solution)/shard_map/ppermute | solution.py:264
  3.5 6.2 %copy-start = (s32[1024]{0:T(1024)S(1)}, s32[1024]{0:T(1024)}, u32[]{:S(2)}) copy-start(s32[1024]{0:T(1024)} %param.13) | copy-start | bytes 12292
  3.5 9.6 %collective-permute-start.4 = (bf16[8,128,128]{2,1,0:T(8,128)(2,1)S(1)}, bf16[8,128,128]{2,1,0:T(8,128)(2,1)S(1)}, u32[]{:S(2)}, u32[]{:S(2)}) collective-permute-start(bf16[8,128,128]{2,1,0:T(8,128)(2,1)S(1)} %pack.1.refs_3_), channel_id=1, source_target_pairs={{0,2},{1,3},{2,4},{3,5},{4,6},{5,7},{8,10},{9,11},{10,12},{11,13},... | collective-permute-start | bytes 786440 | tf_op jit(solution)/shard_map/ppermute | solution.py:268
  11.5 6.7 %collective-permute-start.5 = (bf16[8,128,128]{2,1,0:T(8,128)(2,1)S(1)}, bf16[8,128,128]{2,1,0:T(8,128)(2,1)S(1)}, u32[]{:S(2)}, u32[]{:S(2)}) collective-permute-start(bf16[8,128,128]{2,1,0:T(8,128)(2,1)S(1)} %get-tuple-element.29), channel_id=1, source_target_pairs={{0,4},{1,5},{2,6},{3,7},{8,12},{9,13},{10,14},{11,15},{16,20},{17,... | collective-permute-start | bytes 786440 | tf_op jit(solution)/shard_map/ppermute | solution.py:268
  13.8 6.3 %collective-permute-start.6 = (bf16[8,128,128]{2,1,0:T(8,128)(2,1)S(1)}, bf16[8,128,128]{2,1,0:T(8,128)(2,1)S(1)}, u32[]{:S(2)}, u32[]{:S(2)}) collective-permute-start(bf16[8,128,128]{2,1,0:T(8,128)(2,1)S(1)} %get-tuple-element.31), channel_id=1, source_target_pairs={{4,2},{5,3},{12,10},{13,11},{20,18},{21,19},{28,26},{29,27}} | collective-permute-start | bytes 786440 | tf_op jit(solution)/shard_map/ppermute | solution.py:268
  14.7 11.0 %collective-permute-start.8 = (bf16[8,128,128]{2,1,0:T(8,128)(2,1)S(1)}, bf16[8,128,128]{2,1,0:T(8,128)(2,1)S(1)}, u32[]{:S(2)}, u32[]{:S(2)}) collective-permute-start(bf16[8,128,128]{2,1,0:T(8,128)(2,1)S(1)} %get-tuple-element.35), channel_id=1, source_target_pairs={{2,0},{3,1},{6,4},{7,5},{10,8},{11,9},{14,12},{15,13},{18,16},{19,... | collective-permute-start | bytes 786440 | tf_op jit(solution)/shard_map/ppermute | solution.py:268
  18.9 19.1 %collective-permute-start.9 = (bf16[8,128,128]{2,1,0:T(8,128)(2,1)S(1)}, bf16[8,128,128]{2,1,0:T(8,128)(2,1)S(1)}, u32[]{:S(2)}, u32[]{:S(2)}) collective-permute-start(bf16[8,128,128]{2,1,0:T(8,128)(2,1)S(1)} %get-tuple-element.36), channel_id=1, source_target_pairs={{4,0},{5,1},{6,2},{7,3},{12,8},{13,9},{14,10},{15,11},{20,16},{21,... | collective-permute-start | bytes 786440 | tf_op jit(solution)/shard_map/ppermute | solution.py:268
  21.6 16.5 %collective-permute-start.7 = (bf16[128,32,128]{2,1,0:T(8,128)(2,1)S(1)}, bf16[128,32,128]{2,1,0:T(8,128)(2,1)S(1)}, u32[]{:S(2)}, u32[]{:S(2)}) collective-permute-start(bf16[128,32,128]{2,1,0:T(8,128)(2,1)S(1)} %get-tuple-element.33), channel_id=1, source_target_pairs={{0,1},{1,0},{2,3},{3,2},{4,5},{5,4},{6,7},{7,6},{8,9},{9,8},{10,11... | collective-permute-start | bytes 3145736 | tf_op jit(solution)/shard_map/ppermute | solution.py:264
